TPU v7x, 128 devices: a whole 4x4x4 slice. The times are simulated.
128 devices in a mesh: text: 16 (over y, x), col: 8 (over z, core).
Axes of the slice: x: 4, y: 4, z: 4, core: 2. Of those that a mesh axis runs over, the one named last changes fastest.
Arguments:
- states: bfloat16 [16384, 16, 2048], P(('text', 'col')), may hold values from -6 to 6
- enc_weight: bfloat16 [2048, 1024], replicated, may hold values from -0.125 to 0.125
- self_weight: bfloat16 [1024, 1024], replicated, may hold values from -0.1875 to 0.1875
- neighbour_weight: bfloat16 [1024, 1024], replicated, may hold values from -0.1875 to 0.1875
- edge_weight: bfloat16 [16384, 8, 16, 128], P('text', 'col'), may hold values from 0.099609375 to 1
- tile_live: int32 [128, 8, 16], P('text', 'col'), may hold values from 0 to 1, as said below
- out_grad: bfloat16 [16384, 1024], P(('text', 'col')), may hold values from -6 to 6
- overflow: int32 [1], replicated, may hold values from 0 to 1024
Outputs:
- node_out: bfloat16 [16384, 1024], P(('text', 'col'))
- enc_grad: float32 [2048, 1024], P(('text', 'col'))
Inputs may be any that keep to these rules, and one draw needn't show every extreme that they name: `tile_live`: 0 or 1 for each tile. No bound on how many tiles are live, in all or in any row block, may be relied on.
All inputs are finite; a program needn't handle non-finite values.
Results may differ from a plain program's by a relative error of at most 0.006.
Values may be sent and summed in bfloat16 or wider, within the bound.
A program may use at most 128 MiB of HBM per device.

v0:
```python
import math

import jax
import jax.numpy as jnp
from jax import lax
from jax.sharding import PartitionSpec as P


def local(
    states, enc_weight, self_weight, neighbour_weight, edge_weight, tile_live, out_grad, overflow
):
    blk, seq, width = states.shape
    hid = enc_weight.shape[1]
    flat = states.reshape(blk * seq, width)
    zeta = jnp.dot(flat, enc_weight, preferred_element_type=jnp.float32).reshape(blk, seq, hid)
    squash = jnp.tanh(zeta)
    input_features = jnp.mean(squash, axis=1).astype(jnp.bfloat16)
    rows = edge_weight.shape[0]
    ntext = edge_weight.shape[2]
    tiles = tile_live.shape[0]
    live = tile_live.reshape(tiles, 1, ntext, 1).astype(jnp.bfloat16)
    masked = (edge_weight.reshape(tiles, rows // tiles, ntext, blk) * live).reshape(
        rows, ntext * blk
    )
    local_deg = jnp.sum(masked, axis=1, dtype=jnp.float32)
    columns = masked
    partial_value = jnp.dot(
        columns,
        lax.all_gather(input_features, "text", axis=0, tiled=True),
        preferred_element_type=jnp.float32,
    )
    neighbour_sum, degree_vector = (
        lax.psum_scatter(partial_value, "col", scatter_dimension=0, tiled=True),
        lax.psum_scatter(local_deg, "col", scatter_dimension=0, tiled=True),
    )
    inverse_root_degree = lax.rsqrt(1.0 + degree_vector)
    pooled_neighbours = (neighbour_sum * inverse_root_degree[:, None]).astype(jnp.bfloat16)
    pre = jnp.dot(input_features, self_weight, preferred_element_type=jnp.float32) + jnp.dot(
        pooled_neighbours, neighbour_weight, preferred_element_type=jnp.float32
    )
    node_out = jax.nn.silu(pre).astype(jnp.bfloat16)
    sig = jax.nn.sigmoid(pre)
    preactivation_gradient = (
        out_grad.astype(jnp.float32) * sig * (1.0 + pre * (1.0 - sig))
    ).astype(jnp.bfloat16)
    dself = jnp.dot(preactivation_gradient, self_weight.T, preferred_element_type=jnp.float32)
    pooled_gradient = (
        jnp.dot(preactivation_gradient, neighbour_weight.T, preferred_element_type=jnp.float32)
        * inverse_root_degree[:, None]
    ).astype(jnp.bfloat16)
    gathered = lax.all_gather(pooled_gradient, "col", axis=0, tiled=True)
    columns = masked
    dneigh = lax.psum_scatter(
        lax.dot_general(
            columns, gathered, (((0,), (0,)), ((), ())), preferred_element_type=jnp.float32
        ),
        "text",
        scatter_dimension=0,
        tiled=True,
    )
    dx0 = dself + dneigh
    dzeta = (
        (dx0[:, None, :] / seq * (1.0 - squash * squash))
        .astype(jnp.bfloat16)
        .reshape(blk * seq, hid)
    )
    ntotal = lax.axis_size("text") * lax.axis_size("col")
    raw = lax.psum_scatter(
        lax.dot_general(flat, dzeta, (((0,), (0,)), ((), ())), preferred_element_type=jnp.float32),
        ("text", "col"),
        scatter_dimension=0,
        tiled=True,
    )
    nodes_all = blk * ntotal
    factor = 1024.0 / (1024.0 + overflow[0].astype(jnp.float32))
    enc_grad = raw * factor * (seq / math.sqrt(nodes_all * seq))
    return (node_out, enc_grad)


def solution(mesh):
    in_specs = (
        P(("text", "col"), None, None),
        P(),
        P(),
        P(),
        P("text", "col", None, None),
        P("text", "col", None),
        P(("text", "col"), None),
        P(),
    )
    out_specs = (P(("text", "col"), None), P(("text", "col"), None))
    return jax.shard_map(local, mesh=mesh, in_specs=in_specs, out_specs=out_specs, check_vma=False)
```

profile of v0, /device:TPU:0, one launch (start us, length us, event | category | flops | bytes accessed | tf_op | source)
XLA Modules:
  0.0 952.3 jit_solution(4458916993142733256)
XLA Ops:
  7.2 0.0 all-gather.3.cloned.1.call-start
  7.2 18.3 %tanh_reduce_fusion = (f32[128,1024]{1,0:T(8,128)S(1)}, f32[128,16,1024]{2,0,1:T(8,128)}) fusion(bf16[2048,1024]{1,0:T(8,128)(2,1)} %param.9, bf16[128,16,2048]{2,1,0:T(8,128)(2,1)} %param.8), kind=kOutput, calls=%fused_computation.2 | convolution fusion | flops 8591900672 | bytes 21495808 | tf_op jit(solution)/shard_map/dot_general | solution.py:15
  25.5 0.7 multiply_convert_fusion.5
  26.3 0.0 reduce-scatter.6.cloned.1.call-start
  26.3 53.9 %all-gather.3.cloned.1.call-done = bf16[2048,1024]{1,0:T(8,128)(2,1)} async-done(((bf16[128,1024]{1,0:T(8,128)(2,1)}), bf16[2048,1024]{1,0:T(8,128)(2,1)}) %all-gather.3.cloned.1.call-update) | async-done | bytes 4194320 | tf_op jit(solution)/shard_map/all_gather | solution.py:29
  80.3 0.6 mul.70
  80.9 2.1 copy-done.3
  83.0 1.0 copy-done.2
  84.0 8.6 fusion.13
  92.6 0.0 reduce-scatter.6.cloned.1.call-update
  92.6 0.0 all-gather.5.cloned.1.call-start
  92.7 0.6 copy-done.8
  93.3 0.6 dynamic-slice
  94.5 16.9 %convert_reduce_fusion = f32[1024]{0:T(1024)S(1)} fusion(bf16[1024,1,16,128]{3,2,1,0:T(8,128)(2,1)} %param.12, bf16[1024,16]{1,0:T(8,128)(2,1)S(1)} %bitcast.39), kind=kLoop, calls=%fused_computation.1 | loop fusion | flops 6290432 | bytes 4231168 | tf_op jit(solution)/shard_map/reduce_sum | solution.py:25
  111.4 15.0 %all-reduce = f32[1024]{0:T(1024)S(1)} all-reduce(f32[1024]{0:T(1024)S(1)} %convert_reduce_fusion), channel_id=3, replica_groups=mesh['text'=16,'col'=8] {'col'}, use_global_device_ids=true, to_apply=%region_3.0.clone | all-reduce | flops 1024 | bytes 8192
  126.4 0.1 fusion.15
  126.5 2.0 fusion.17
  128.5 2.2 reduce-scatter.6.cloned.1.call-done
  130.8 2.3 multiply_convert_fusion.3
  133.1 0.8 copy-done.9
  133.9 1.6 fusion.11
  135.5 0.2 reduce-scatter.8.cloned.1.call-start
  135.8 24.1 %all-gather.5.cloned.1.call-done = bf16[1024,1024]{1,0:T(8,128)(2,1)} async-done(((bf16[128,1024]{1,0:T(8,128)(2,1)}), bf16[1024,1024]{1,0:T(8,128)(2,1)}) %all-gather.5.cloned.1.call-update) | async-done | bytes 2097168 | tf_op jit(solution)/shard_map/all_gather | solution.py:51
  159.9 12.5 %fusion.12 = f32[2048,1024]{1,0:T(8,128)} fusion(bf16[1024,1024]{1,0:T(8,128)(2,1)} %all-gather.5.cloned.1.call-done, bf16[128,8,16,128]{3,2,1,0:T(8,128)(2,1)} %bitcast.38, bf16[128,8,16,128]{3,2,1,0:T(8,128)(2,1)} %bitcast.35), kind=kOutput, calls=%fused_computation.17 | convolution fusion | flops 4297064448 | bytes 18874368 | tf_op jit(solution)/shard_map/dot_general | solution.py:54
  172.5 0.0 reduce-scatter.10.cloned.1.call-start
  172.5 85.4 %reduce-scatter.8.cloned.1.call-done = f32[128,1024]{1,0:T(8,128)} async-done(((f32[2048,1024]{1,0:T(8,128)}), f32[128,1024]{1,0:T(8,128)}) %reduce-scatter.8.cloned.1.call-update) | async-done | bytes 524304 | tf_op jit(solution)/shard_map/reduce_scatter | solution.py:53
  257.9 1.9 fusion.10
  259.8 24.7 %fusion.4 = f32[2048,1024]{0,1:T(8,128)} fusion(bf16[128,16,2048]{2,1,0:T(8,128)(2,1)} %param.8, f32[128,16,1024]{2,0,1:T(8,128)} %get-tuple-element.7, f32[128,1024]{1,0:T(8,128)S(1)} %fusion.10), kind=kOutput, calls=%fused_computation.7 | convolution fusion | flops 8598323200 | bytes 25690112 | tf_op jit(solution)/shard_map/dot_general | solution.py:69
  284.5 9.3 copy.21
  294.7 649.2 %reduce-scatter.10.cloned.1.call-done = f32[16,1024]{1,0:T(8,128)} async-done(((f32[2048,1024]{1,0:T(8,128)}), f32[16,1024]{1,0:T(8,128)}) %reduce-scatter.10.cloned.1.call-update) | async-done | bytes 65552
  943.9 1.0 copy.22
  945.0 0.8 copy.19
  (25 shorter events, 0.2 us)
Async XLA Ops:
  7.2 123.6 %copy-start = (bf16[1024,1024]{1,0:T(8,128)(2,1)S(1)}, bf16[1024,1024]{1,0:T(8,128)(2,1)}, u32[]{:S(2)}) copy-start(bf16[1024,1024]{1,0:T(8,128)(2,1)} %param.11) | copy-start | bytes 6291460
  7.2 19.1 %copy-start.6 = (s32[8,1,16]{2,1,0:T(1,128)S(1)}, s32[8,1,16]{2,1,0:T(1,128)}, u32[]{:S(2)}) copy-start(s32[8,1,16]{2,1,0:T(1,128)} %param.13) | copy-start | bytes 1540
  7.2 73.1 %all-gather.3.cloned.1.call-start = ((), (), s32[]{:S(2)}) async-start(), calls=%async_computation.3 | async-start | bytes 4456448 | tf_op jit(solution)/shard_map/all_gather | solution.py:29
  26.3 104.5 %reduce-scatter.6.cloned.1.call-start = ((), (), s32[]{:S(2)}) async-start(), calls=%async_computation.4 | async-start | bytes 4718592 | tf_op jit(solution)/shard_map/reduce_scatter | solution.py:33
  80.3 3.7 copy-start.2
  80.9 2.1 copy-start.3
  92.6 0.7 copy-start.8
  92.6 33.9 %copy-start.4 = (bf16[128,1024]{1,0:T(8,128)(2,1)S(1)}, bf16[128,1024]{1,0:T(8,128)(2,1)}, u32[]{:S(2)}) copy-start(bf16[128,1024]{1,0:T(8,128)(2,1)} %multiply_convert_fusion.5) | copy-start | bytes 786436
  92.6 67.3 %all-gather.5.cloned.1.call-start = ((), (), s32[]{:S(2)}) async-start(), calls=%async_computation.5 | async-start | bytes 2359296 | tf_op jit(solution)/shard_map/all_gather | solution.py:51
  111.4 22.5 %copy-start.7 = (bf16[128,1024]{1,0:T(8,128)(2,1)S(1)}, bf16[128,1024]{1,0:T(8,128)(2,1)}, u32[]{:S(2)}) copy-start(bf16[128,1024]{1,0:T(8,128)(2,1)} %param.14) | copy-start | bytes 786436
  133.1 0.8 copy-start.9
  135.5 122.4 %reduce-scatter.8.cloned.1.call-start = ((), (), s32[]{:S(2)}) async-start(), calls=%async_computation.6 | async-start | bytes 8912896 | tf_op jit(solution)/shard_map/reduce_scatter | solution.py:53
  172.4 85.5 %copy-start.5 = (bf16[1024,1024]{1,0:T(8,128)(2,1)S(1)}, bf16[1024,1024]{1,0:T(8,128)(2,1)}, u32[]{:S(2)}) copy-start(bf16[1024,1024]{1,0:T(8,128)(2,1)} %param.10) | copy-start | bytes 6291460
  172.4 85.5 %copy-start.10 = (f32[128,1024]{1,0:T(8,128)S(1)}, f32[128,1024]{1,0:T(8,128)}, u32[]{:S(2)}) copy-start(f32[128,1024]{1,0:T(8,128)} %copy-done.9) | copy-start | bytes 1572868
  172.5 771.4 %reduce-scatter.10.cloned.1.call-start = ((), (), s32[]{:S(2)}) async-start(), calls=%async_computation.7 | async-start | bytes 8454144
  293.8 652.0 %copy-start.1 = (bf16[1024,1024]{1,0:T(8,128)(2,1)S(1)}, bf16[1024,1024]{1,0:T(8,128)(2,1)}, u32[]{:S(2)}) copy-start(bf16[1024,1024]{1,0:T(8,128)(2,1)} %param.11) | copy-start | bytes 6291460
Sparse Core Ops, SparseCore 0:
  26.4 53.8 all-gather.2
  92.8 37.9 reduce-scatter.5
  135.7 24.2 all-gather.4
  172.6 85.2 reduce-scatter.7
  294.0 649.9 reduce-scatter.9
where the time goes:
time: 953 us; the launch traced here: 952 us
  waiting for transfers between devices  815 us (86%)
  matrix products  72 us (8%)
  other arithmetic  17.7 us (2%)
  local copies, waits for them, and re-layouts  16.8 us (2%)
  between operations  15.4 us (2%)
  blocking collectives  15 us (2%)
    unnamed x6, waiting for transfers between devices  649 us
    reduce_scatter x1, waiting for transfers between devices, local(): lax.psum_scatter(lax.dot_general(columns, gathered, (((0,), (0,)), ((), (...  85.4 us
    all_gather x1, waiting for transfers between devices, local(): lax.all_gather(input_features, 'text', axis=0, tiled=True)  53.9 us
    dot_general x1, matrix products, local(): lax.dot_general(flat, dzeta, (((0,), (0,)), ((), ())), preferred_element_...  24.7 us
    all_gather x1, waiting for transfers between devices, local(): gathered = lax.all_gather(pooled_gradient, 'col', axis=0, tiled=True)  24.1 us
  transfers between devices with their start and end apart: 5, of which 5 were waited for; matrix products, arithmetic and copies ran while one was open for 2% of the time, Pallas kernels for 0%

commit v1 on v0

v1 whole, which is shorter than its diff:
```python
import math

import jax
import jax.numpy as jnp
from jax import lax
from jax.experimental import pallas as pl
from jax.experimental.pallas import tpu as pltpu
from jax.sharding import PartitionSpec as P

MESH = pl.DeviceIdType.MESH
BF = jnp.bfloat16
F32 = jnp.float32
NC = 4
W = 256
STEPS = (1, 2, 3)


def dot(a, b):
    return jnp.dot(a, b, preferred_element_type=F32)


def dot_nt(a, b):
    return lax.dot_general(a, b, (((1,), (1,)), ((), ())), preferred_element_type=F32)


def kernel(
    states_h, enc_h, self_h, neigh_h, edge_h, grad_h, live, overflow,
    node_out, enc_grad,
    states, enc, w_self, w_neigh, edge, edge_f, adj, squash, feats, part, out_grad,
    core_out, core_in, zed_out, zed_in, deg_out, deg_in,
    pre, dagg, dself, hop1_in, keep, hop2_in, dzeta, rcore_in, rzed_in, rx_in, ry_in,
    sums, last,
    load_sem, ag_s, ag_r, deg_s, deg_r, core_s, core_r, zed_s, zed_r, dg_s, dg_r, fw_s, fw_r,
    h1_s, h1_r, h2_s, h2_r, rc_s, rc_r, rz_s, rz_r, rx_s, rx_r, ry_s, ry_r,
):
    t = lax.axis_index("text")
    c = lax.axis_index("col")
    y, x, z, k = t // 4, t % 4, c // 2, c % 2
    other = 1 - k

    def at_x(d):
        return (y * 4 + (x + d) % 4, c)

    def at_y(d):
        return (((y + d) % 4) * 4 + x, c)

    def at_z(d):
        return (t, ((z + d) % 4) * 2 + k)

    def at_col(d):
        return (t, (c + d) % 8)

    sibling = (t, z * 2 + other)

    def send(src, dst, ssem, rsem, to):
        copy = pltpu.make_async_remote_copy(
            src_ref=src, dst_ref=dst, send_sem=ssem, recv_sem=rsem, device_id=to,
            device_id_type=MESH,
        )
        copy.start()
        return copy

    def load_states(m):
        rows = pl.ds(m * 256, 256)
        return pltpu.make_async_copy(states_h.at[rows], states.at[rows], load_sem.at[m])

    def load_enc(j):
        return pltpu.make_async_copy(enc_h.at[:, pl.ds(j * W, W)], enc.at[j], load_sem.at[8 + j])

    load_enc(0).start()
    for m in range(8):
        load_states(m).start()
    for j in range(1, NC):
        load_enc(j).start()
    rest = [
        pltpu.make_async_copy(src, dst, load_sem.at[12 + n])
        for n, (src, dst) in enumerate(
            [(edge_h, edge), (self_h, w_self), (neigh_h, w_neigh), (grad_h, out_grad)]
        )
    ]
    for copy in rest:
        copy.start()

    barrier = pltpu.get_barrier_semaphore()
    for d in STEPS:
        pl.semaphore_signal(barrier, inc=1, device_id=at_x(d), device_id_type=MESH)
        pl.semaphore_signal(barrier, inc=1, device_id=at_y(d), device_id_type=MESH)
    for d in range(1, 8):
        pl.semaphore_signal(barrier, inc=1, device_id=at_col(d), device_id_type=MESH)

    def encode(j):
        load_enc(j).wait()

        def tile(m, _):
            rows = pl.ds(m * 256, 256)
            if j == 0:
                load_states(m).wait()
            s = jnp.tanh(dot(states[rows, :], enc[j]))
            squash[j, rows, :] = s
            mean = jnp.sum(s.reshape(16, 16, W), axis=1) * (1.0 / 16.0)
            feats[j, y, x, pl.ds(m * 16, 16), :] = mean.astype(BF)
            return 0

        lax.fori_loop(0, 8, tile, 0)

    LO, HI = pl.ds(0, 64), pl.ds(64, 64)

    def gather1(j):
        own_a, own_b = feats.at[j, y, x, LO], feats.at[j, y, x, HI]
        return [
            send(own_a, own_a, ag_s.at[j, d - 1], ag_r.at[j, d - 1], at_x(d)) for d in STEPS
        ] + [
            send(own_b, own_b, ag_s.at[j, 2 + d], ag_r.at[j, 2 + d], at_y(d)) for d in STEPS
        ]

    def gather2(j, first):
        for copy in first[:3]:
            copy.wait_recv()
        row = feats.at[j, y, :, LO]
        out = [
            send(row, row, ag_s.at[j, 5 + d], ag_r.at[j, 5 + d], at_y(d)) for d in STEPS
        ]
        for copy in first[3:]:
            copy.wait_recv()
        column = feats.at[j, :, x, HI]
        return out + [
            send(column, column, ag_s.at[j, 8 + d], ag_r.at[j, 8 + d], at_x(d)) for d in STEPS
        ]

    def adjacency(r, _):
        rows = pl.ds(r * 128, 128)
        edge_f[...] = edge[rows].astype(F32).reshape(2048, 128)
        total = jnp.zeros((128, 128), F32)
        for i in range(16):
            a = edge_f[pl.ds(i, 128, stride=16), :] * live[r, i].astype(F32)
            adj[rows, i * 128 : (i + 1) * 128] = a.astype(BF)
            total = total + a
        column = jnp.broadcast_to(jnp.sum(total, axis=1, keepdims=True), (128, 128))
        deg_out[r] = column.T[0:8, :]
        return 0

    def aggregate(j, second):
        for copy in second:
            copy.wait_recv()
        slot = j % 2
        chunk = feats[j].reshape(2048, W)

        def tile(q, _):
            rows = pl.ds(q * 256, 256)
            part[slot, q] = dot(adj[rows, :], chunk).reshape(2, 128, W)
            core_out[j, q] = part[slot, q, other].astype(BF)
            return 0

        lax.fori_loop(0, 4, tile, 0)
        return send(core_out.at[j], core_in.at[j], core_s.at[j], core_r.at[j], sibling)

    def column_sum(j, copy):
        copy.wait_recv()
        for q in range(4):
            part[j % 2, q, k] = part[j % 2, q, k] + core_in[j, q].astype(F32)
            zed_out[j, q] = part[j % 2, q, k].astype(BF)
        return [
            send(
                zed_out.at[j, (z + d) % 4], zed_in.at[j, d - 1],
                zed_s.at[j, d - 1], zed_r.at[j, d - 1], at_z(d),
            )
            for d in STEPS
        ]

    def combine(j, copies, scale):
        for copy in copies:
            copy.wait_recv()
        total = part[j % 2, z, k]
        for d in range(3):
            total = total + zed_in[j, d].astype(F32)
        pooled = (total * scale).astype(BF)
        rows = pl.ds(j * W, W)
        term = dot(feats[j, y, x], w_self[rows, :]) + dot(pooled, w_neigh[rows, :])
        pre[...] = term if j == 0 else pre[...] + term

    sends = []
    encode(0)
    pl.semaphore_wait(barrier, 13)
    first, second = [gather1(0)], []
    for j in range(1, NC):
        encode(j)
        first.append(gather1(j))
        second.append(gather2(j - 1, first[j - 1]))
    rest[0].wait()
    second.append(gather2(NC - 1, first[NC - 1]))
    lax.fori_loop(0, 8, adjacency, 0)
    deg_copies = [
        send(
            deg_out.at[(c + d) % 8], deg_in.at[d - 1], deg_s.at[d - 1], deg_r.at[d - 1], at_col(d)
        )
        for d in range(1, 8)
    ]

    def flip(m, _):
        def pair(n, _):
            a, b = pl.ds(m * 256, 256), pl.ds(n * 256, 256)
            up, down = states[a, b], states[b, a]
            states[a, b] = down.T
            states[b, a] = up.T
            return 0

        lax.fori_loop(0, m + 1, pair, 0)
        return 0

    lax.fori_loop(0, 8, flip, 0)

    for copy in deg_copies:
        copy.wait_recv()
    degree = deg_out[c]
    for d in range(7):
        degree = degree + deg_in[d]
    inv_row = lax.rsqrt(1.0 + degree)[0:1, :]
    inv_column = jnp.broadcast_to(inv_row, (128, 128)).T[:, 0:1]

    for copy in rest[1:]:
        copy.wait()
    core, zed = [], []
    for j in range(NC):
        core.append(aggregate(j, second[j]))
        zed.append(column_sum(j, core[j]))
        if j >= 1:
            combine(j - 1, zed[j - 1], inv_column)
    combine(NC - 1, zed[NC - 1], inv_column)

    v = pre[...]
    sg = 1.0 / (1.0 + jnp.exp(-v))
    node_out[...] = (v * sg).astype(BF)
    dpre = (out_grad[...].astype(F32) * sg * (1.0 + v * (1.0 - sg))).astype(BF)

    around = []
    for j in range(NC):
        rows = pl.ds(j * W, W)
        dagg[j, c] = (dot_nt(w_neigh[rows, :], dpre) * inv_row).astype(BF)
        own = dagg.at[j, c]
        around.append(
            [send(own, own, dg_s.at[j, d - 1], dg_r.at[j, d - 1], at_z(d)) for d in STEPS]
            + [send(own, own, dg_s.at[j, 3], dg_r.at[j, 3], sibling)]
        )
    for j in range(NC):
        dself[j] = dot_nt(w_self[pl.ds(j * W, W), :], dpre)

    for copies in first + second + zed:
        for copy in copies:
            copy.wait_send()
    for copy in core + deg_copies:
        copy.wait_send()

    A, B = pl.ds(0, 128), pl.ds(128, 128)

    def forward(j):
        out = []
        for d in STEPS:
            around[j][d - 1].wait_recv()
            block = dagg.at[j, ((z - d + 4) % 4) * 2 + k]
            out.append(send(block, block, fw_s.at[j, d - 1], fw_r.at[j, d - 1], sibling))
        return out

    def scatter1(j, passed):
        around[j][3].wait_recv()
        for copy in passed:
            copy.wait_recv()
        chunk = jnp.concatenate([dagg[j, q] for q in range(8)], axis=1)

        def tile(n, _):
            p = dot(chunk, adj[:, pl.ds(pl.multiple_of(n * 256, 256), 256)]).astype(BF)
            for i in range(2):
                block = p[:, i * 128 : (i + 1) * 128]
                yy, xx = n // 2, (n % 2) * 2 + i
                feats[j, yy, xx, :, 0:128] = block[0:128]
                feats[j, yy, xx, :, 128:256] = block[128:256]
            return 0

        lax.fori_loop(0, 8, tile, 0)
        out = []
        for d in STEPS:
            out.append(
                send(
                    feats.at[j, (y + d) % 4, :, :, A], hop1_in.at[j, 0, d - 1],
                    h1_s.at[j, d - 1], h1_r.at[j, d - 1], at_y(d),
                )
            )
            out.append(
                send(
                    feats.at[j, :, (x + d) % 4, :, B], hop1_in.at[j, 1, d - 1],
                    h1_s.at[j, 2 + d], h1_r.at[j, 2 + d], at_x(d),
                )
            )
        return out

    def scatter2(j, copies):
        for copy in copies:
            copy.wait_recv()
        for q in range(4):
            a = feats[j, y, q, :, 0:128].astype(F32)
            b = feats[j, q, x, :, 128:256].astype(F32)
            for d in range(3):
                a = a + hop1_in[j, 0, d, q].astype(F32)
                b = b + hop1_in[j, 1, d, q].astype(F32)
            part[0, q, 0, :, 0:128] = a
            part[0, q, 0, :, 128:256] = b
            core_out[j, q, :, 0:128] = a.astype(BF)
            core_out[j, q, :, 128:256] = b.astype(BF)
        keep[j, 0] = part[0, x, 0, :, 0:128]
        keep[j, 1] = part[0, y, 0, :, 128:256]
        out = []
        for d in STEPS:
            out.append(
                send(
                    core_out.at[j, (x + d) % 4, :, A], hop2_in.at[j, 0, d - 1],
                    h2_s.at[j, d - 1], h2_r.at[j, d - 1], at_x(d),
                )
            )
            out.append(
                send(
                    core_out.at[j, (y + d) % 4, :, B], hop2_in.at[j, 1, d - 1],
                    h2_s.at[j, 2 + d], h2_r.at[j, 2 + d], at_y(d),
                )
            )
        return out

    def encoder_term(j, copies):
        for copy in copies:
            copy.wait_recv()
        halves = []
        for h in range(2):
            total = keep[j, h]
            for d in range(3):
                total = total + hop2_in[j, h, d].astype(F32)
            halves.append(total)
        dx0 = jnp.concatenate(halves, axis=0) + dself[j]
        part[1, 0, 0] = dx0.T * (1.0 / 16.0)

        def tile(m, _):
            rows = pl.ds(m * 256, 256)
            s = squash[j, rows, :].reshape(16, 16, W)
            g = part[1, 0, 0, pl.ds(m * 16, 16), :].reshape(16, 1, W)
            dzeta[rows, :] = (g * (1.0 - s * s)).astype(BF).reshape(256, W)
            return 0

        lax.fori_loop(0, 8, tile, 0)

        def term(m, _):
            rows = pl.ds(m * 256, 256)
            squash[j, rows, :] = dot(states[rows, :], dzeta[...])
            for g in range(8):
                away = squash[j, pl.ds(m * 256 + g * 32 + other * 16, 16), :].astype(BF)
                enc[j, pl.ds(m * 128 + g * 16, 16), :] = away
            return 0

        lax.fori_loop(0, 8, term, 0)
        return send(
            enc.at[j, pl.ds(0, 1024)], rcore_in.at[j], rc_s.at[j], rc_r.at[j], sibling
        )

    def term_zed(j, copy):
        copy.wait_recv()

        def tile(m, _):
            for q in range(4):
                g = m * 4 + q
                mine = pl.ds(g * 32 + k * 16, 16)
                total = squash[j, mine, :] + rcore_in[j, pl.ds(g * 16, 16), :].astype(F32)
                squash[j, mine, :] = total
                enc[j, pl.ds(1024 + q * 256 + m * 16, 16), :] = total.astype(BF)
            return 0

        lax.fori_loop(0, 16, tile, 0)
        return [
            send(
                enc.at[j, pl.ds(1024 + ((z + d) % 4) * 256, 256)], rzed_in.at[j, d - 1],
                rz_s.at[j, d - 1], rz_r.at[j, d - 1], at_z(d),
            )
            for d in STEPS
        ]

    def term_x(j, copies):
        for copy in copies:
            copy.wait_recv()

        def tile(m, _):
            total = squash[j, pl.ds((m * 4 + z) * 32 + k * 16, 16), :]
            for d in range(3):
                total = total + rzed_in[j, d, pl.ds(m * 16, 16), :].astype(F32)
            rx_out = pl.ds((m % 4) * 64 + (m // 4) * 16, 16)
            sums[j, rx_out, :] = total
            return 0

        lax.fori_loop(0, 16, tile, 0)
        return [
            send(
                sums.at[j, pl.ds(((x + d) % 4) * 64, 64)], rx_in.at[j, d - 1],
                rx_s.at[j, d - 1], rx_r.at[j, d - 1], at_x(d),
            )
            for d in STEPS
        ]

    def term_y(j, copies):
        for copy in copies:
            copy.wait_recv()
        total = sums[j, pl.ds(x * 64, 64), :]
        for d in range(3):
            total = total + rx_in[j, d]
        last[j] = total
        return [
            send(
                last.at[j, pl.ds(((y + d) % 4) * 16, 16)], ry_in.at[j, d - 1],
                ry_s.at[j, d - 1], ry_r.at[j, d - 1], at_y(d),
            )
            for d in STEPS
        ]

    factor = 1024.0 / (1024.0 + overflow[0].astype(F32)) * (16.0 / math.sqrt(16384 * 16))

    def finish(j, copies):
        for copy in copies:
            copy.wait_recv()
        total = last[j, pl.ds(y * 16, 16), :]
        for d in range(3):
            total = total + ry_in[j, d]
        enc_grad[:, j * W : (j + 1) * W] = total * factor

    passed, hop1, hop2 = [forward(0)], [], []
    for j in range(NC - 1):
        passed.append(forward(j + 1))
        hop1.append(scatter1(j, passed[j]))
    hop2.append(scatter2(0, hop1[0]))
    hop1.append(scatter1(NC - 1, passed[NC - 1]))
    rcore, rzed, rx, ry = [], [], [], []
    for j in range(NC):
        rcore.append(encoder_term(j, hop2[j]))
        if j + 1 < NC:
            hop2.append(scatter2(j + 1, hop1[j + 1]))
        if j >= 1:
            rzed.append(term_zed(j - 1, rcore[j - 1]))
        if j >= 2:
            rx.append(term_x(j - 2, rzed[j - 2]))
        if j >= 3:
            ry.append(term_y(j - 3, rx[j - 3]))
    rzed.append(term_zed(NC - 1, rcore[NC - 1]))
    rx.append(term_x(NC - 2, rzed[NC - 2]))
    ry.append(term_y(NC - 3, rx[NC - 3]))
    finish(0, ry[0])
    rx.append(term_x(NC - 1, rzed[NC - 1]))
    ry.append(term_y(NC - 2, rx[NC - 2]))
    finish(1, ry[1])
    ry.append(term_y(NC - 1, rx[NC - 1]))
    finish(2, ry[2])
    finish(3, ry[3])

    for copies in around + passed + hop1 + hop2 + rzed + rx + ry:
        for copy in copies:
            copy.wait_send()
    for copy in rcore:
        copy.wait_send()


def local(
    states, enc_weight, self_weight, neighbour_weight, edge_weight, tile_live, out_grad, overflow
):
    states = states.reshape(2048, 2048)
    edge_weight = edge_weight.reshape(1024, 16, 128)
    tile_live = tile_live.reshape(8, 16)
    hbm = pl.BlockSpec(memory_space=pl.ANY)
    smem = pl.BlockSpec(memory_space=pltpu.SMEM)
    vmem = pl.BlockSpec(memory_space=pltpu.VMEM)
    V, S = pltpu.VMEM, pltpu.SemaphoreType.DMA
    buffers = [
        V((2048, 2048), BF),
        V((NC, 2048, W), BF),
        V((1024, 1024), BF),
        V((1024, 1024), BF),
        V((1024, 16, 128), BF),
        V((2048, 128), F32),
        V((1024, 2048), BF),
        V((NC, 2048, W), F32),
        V((NC, 4, 4, 128, W), BF),
        V((2, 4, 2, 128, W), F32),
        V((128, 1024), BF),
        V((NC, 4, 128, W), BF),
        V((NC, 4, 128, W), BF),
        V((NC, 4, 128, W), BF),
        V((NC, 3, 128, W), BF),
        V((8, 8, 128), F32),
        V((7, 8, 128), F32),
        V((128, 1024), F32),
        V((NC, 8, W, 128), BF),
        V((NC, W, 128), F32),
        V((NC, 2, 3, 4, 128, 128), BF),
        V((NC, 2, 128, 128), F32),
        V((NC, 2, 3, 128, 128), BF),
        V((2048, W), BF),
        V((NC, 1024, W), BF),
        V((NC, 3, 256, W), BF),
        V((NC, 3, 64, W), F32),
        V((NC, 3, 16, W), F32),
        V((NC, 256, W), F32),
        V((NC, 64, W), F32),
    ]
    shapes = [
        (NC, 12), (7,), (NC,), (NC, 3), (NC, 4), (NC, 3), (NC, 6), (NC, 6), (NC,), (NC, 3),
        (NC, 3), (NC, 3),
    ]
    semaphores = [S((16,))] + [S(shape) for shape in shapes for _ in range(2)]
    return pl.pallas_call(
        kernel,
        out_shape=(
            jax.ShapeDtypeStruct((128, 1024), BF),
            jax.ShapeDtypeStruct((16, 1024), F32),
        ),
        in_specs=[hbm] * 6 + [smem] * 2,
        out_specs=(vmem, vmem),
        scratch_shapes=buffers + semaphores,
        compiler_params=pltpu.CompilerParams(
            collective_id=0, has_side_effects=True, vmem_limit_bytes=63 * 1024 * 1024
        ),
        name="step",
    )(states, enc_weight, self_weight, neighbour_weight, edge_weight, out_grad, tile_live, overflow)


def solution(mesh):
    in_specs = (
        P(("text", "col"), None, None),
        P(),
        P(),
        P(),
        P("text", "col", None, None),
        P("text", "col", None),
        P(("text", "col"), None),
        P(),
    )
    out_specs = (P(("text", "col"), None), P(("text", "col"), None))
    return jax.shard_map(local, mesh=mesh, in_specs=in_specs, out_specs=out_specs, check_vma=False)
```

time: 953 us -> 156 us (0.16)
  waiting for transfers between devices: 815 us -> 0 us
  Pallas kernels: 0 us -> 151 us
  matrix products: 72 us -> 0 us
  other arithmetic: 17.7 us -> 0 us
  blocking collectives: 15 us -> 0 us
  between operations: 15.4 us -> 1.29 us
  local copies, waits for them, and re-layouts: 16.8 us -> 3.14 us
    unnamed x6 -> x0, waiting for transfers between devices: 649 us -> none
    pallas_call x0 -> x1, Pallas kernels: none -> 151 us  [local(): pl.pallas_call(kernel, out_shape=(jax.ShapeDtypeStruct((128, 1024), BF),...]
    reduce_scatter x2 -> x0, waiting for transfers between devices: 87.6 us -> none  [the longest x1 85.4 us: local(): lax.psum_scatter(lax.dot_general(columns, gathered, (((0,), (0,)), ((), (...]
    all_gather x2 -> x0, waiting for transfers between devices: 78.1 us -> none  [the longest x1 53.9 us: local(): lax.all_gather(input_features, 'text', axis=0, tiled=True)]
    dot_general x8 -> x0, matrix products: 72 us -> none  [the longest x1 24.7 us: local(): lax.dot_general(flat, dzeta, (((0,), (0,)), ((), ())), preferred_element_...]
    reduce_sum x1 -> x0, other arithmetic: 16.9 us -> none  [local(): local_deg = jnp.sum(masked, axis=1, dtype=jnp.float32)]
    unnamed x1 -> x0, blocking collectives: 15 us -> none
    unnamed x26 -> x2, local copies, waits for them, and re-layouts: 16.2 us -> 3.14 us
  transfers between devices with their start and end apart: 5 -> 0, of which waited for: 5 -> 0; matrix products, arithmetic and copies ran while one was open for 2% -> 0% of each run, Pallas kernels for 0% -> 0%
where the time goes in v1:
time: 156 us; the launch traced here: 155 us
  Pallas kernels  151 us (97%)
  local copies, waits for them, and re-layouts  3.14 us (2%)
    pallas_call x1, Pallas kernels, local(): pl.pallas_call(kernel, out_shape=(jax.ShapeDtypeStruct((128, 1024), BF),...  151 us
    unnamed x2, local copies, waits for them, and re-layouts  3.14 us

profile of v1, /device:TPU:0, one launch (start us, length us, event | category | flops | bytes accessed | tf_op | source)
XLA Modules:
  0.0 155.3 jit_solution(7352073126821059251)
XLA Ops:
  1.3 150.9 %step.1 = (bf16[128,1024]{1,0:T(8,128)(2,1)}, f32[16,1024]{1,0:T(8,128)}) custom-call(bf16[2048,2048]{1,0:T(8,128)(2,1)} %bitcast.3, bf16[2048,1024]{1,0:T(8,128)(2,1)} %enc_h.1, bf16[1024,1024]{1,0:T(8,128)(2,1)} %self_h.1, bf16[1024,1024]{1,0:T(8,128)(2,1)} %neigh_h.1, bf16[1024,16,128]{2,1,0:T(8,128)(2,1)} %bitcast.4, bf16[128,1024]{1,0:T(8,128)(2,1)} %grad_h.1, ...), custom_call_target="tpu_custom_call" | custom-call | tf_op jit(solution)/shard_map/step/pallas_call | solution.py:509
  152.2 1.7 %copy.13 = bf16[128,1024]{1,0:T(8,128)(2,1)} copy(bf16[128,1024]{1,0:T(8,128)(2,1)} %get-tuple-element.4) | data formatting | bytes 524288
  153.9 1.5 copy.14

commit v2 on v1

--- a/solution.py
+++ b/solution.py
@@ -29,7 +29,7 @@
     states, enc, w_self, w_neigh, edge, edge_f, adj, squash, feats, part, out_grad,
     core_out, core_in, zed_out, zed_in, deg_out, deg_in,
     pre, dagg, dself, hop1_in, keep, hop2_in, dzeta, rcore_in, rzed_in, rx_in, ry_in,
-    sums, last,
+    sums, sums_out, last,
     load_sem, ag_s, ag_r, deg_s, deg_r, core_s, core_r, zed_s, zed_r, dg_s, dg_r, fw_s, fw_r,
     h1_s, h1_r, h2_s, h2_r, rc_s, rc_r, rz_s, rz_r, rx_s, rx_r, ry_s, ry_r,
 ):
@@ -52,11 +52,14 @@
 
     sibling = (t, z * 2 + other)
 
-    def send(src, dst, ssem, rsem, to):
-        copy = pltpu.make_async_remote_copy(
+    def describe(src, dst, ssem, rsem, to):
+        return pltpu.make_async_remote_copy(
             src_ref=src, dst_ref=dst, send_sem=ssem, recv_sem=rsem, device_id=to,
             device_id_type=MESH,
         )
+
+    def send(src, dst, ssem, rsem, to):
+        copy = describe(src, dst, ssem, rsem, to)
         copy.start()
         return copy
 
@@ -91,17 +94,20 @@
     def encode(j):
         load_enc(j).wait()
 
+        size = 512 if j == 0 else 1024
+
         def tile(m, _):
-            rows = pl.ds(m * 256, 256)
+            rows = pl.ds(m * size, size)
             if j == 0:
-                load_states(m).wait()
+                load_states(2 * m).wait()
+                load_states(2 * m + 1).wait()
             s = jnp.tanh(dot(states[rows, :], enc[j]))
             squash[j, rows, :] = s
-            mean = jnp.sum(s.reshape(16, 16, W), axis=1) * (1.0 / 16.0)
-            feats[j, y, x, pl.ds(m * 16, 16), :] = mean.astype(BF)
+            mean = jnp.sum(s.reshape(size // 16, 16, W), axis=1) * (1.0 / 16.0)
+            feats[j, y, x, pl.ds(m * (size // 16), size // 16), :] = mean.astype(BF)
             return 0
 
-        lax.fori_loop(0, 8, tile, 0)
+        lax.fori_loop(0, 2048 // size, tile, 0)
 
     LO, HI = pl.ds(0, 64), pl.ds(64, 64)
 
@@ -118,14 +124,28 @@
             copy.wait_recv()
         row = feats.at[j, y, :, LO]
         out = [
-            send(row, row, ag_s.at[j, 5 + d], ag_r.at[j, 5 + d], at_y(d)) for d in STEPS
+            send(row, row, ag_s.at[j, 6 + n], ag_r.at[j, 6 + n], at_y(d))
+            for n, d in enumerate((1, 3))
         ]
         for copy in first[3:]:
             copy.wait_recv()
         column = feats.at[j, :, x, HI]
         return out + [
-            send(column, column, ag_s.at[j, 8 + d], ag_r.at[j, 8 + d], at_x(d)) for d in STEPS
+            send(column, column, ag_s.at[j, 8 + n], ag_r.at[j, 8 + n], at_x(d))
+            for n, d in enumerate((1, 3))
         ]
+
+    def gather3(j, second):
+        out = []
+        for n, d in enumerate((1, 3)):
+            half = pl.ds(2 * n, 2)
+            second[n].wait_recv()
+            row = feats.at[j, (y + 4 - d) % 4, half, LO]
+            out.append(send(row, row, ag_s.at[j, 10 + n], ag_r.at[j, 10 + n], at_y(d)))
+            second[2 + n].wait_recv()
+            column = feats.at[j, half, (x + 4 - d) % 4, HI]
+            out.append(send(column, column, ag_s.at[j, 12 + n], ag_r.at[j, 12 + n], at_x(d)))
+        return out
 
     def adjacency(r, _):
         rows = pl.ds(r * 128, 128)
@@ -139,26 +159,19 @@
         deg_out[r] = column.T[0:8, :]
         return 0
 
-    def aggregate(j, second):
-        for copy in second:
-            copy.wait_recv()
-        slot = j % 2
-        chunk = feats[j].reshape(2048, W)
-
-        def tile(q, _):
-            rows = pl.ds(q * 256, 256)
-            part[slot, q] = dot(adj[rows, :], chunk).reshape(2, 128, W)
-            core_out[j, q] = part[slot, q, other].astype(BF)
-            return 0
-
-        lax.fori_loop(0, 4, tile, 0)
+    def aggregate(j, third):
+        for copy in third:
+            copy.wait_recv()
+        p = dot(adj[...], feats[j].reshape(2048, W)).reshape(4, 2, 128, W)
+        part[j] = jnp.where(k == 0, p[:, 0], p[:, 1])
+        core_out[j] = jnp.where(k == 0, p[:, 1], p[:, 0]).astype(BF)
         return send(core_out.at[j], core_in.at[j], core_s.at[j], core_r.at[j], sibling)
 
     def column_sum(j, copy):
         copy.wait_recv()
         for q in range(4):
-            part[j % 2, q, k] = part[j % 2, q, k] + core_in[j, q].astype(F32)
-            zed_out[j, q] = part[j % 2, q, k].astype(BF)
+            part[j, q] = part[j, q] + core_in[j, q].astype(F32)
+            zed_out[j, q] = part[j, q].astype(BF)
         return [
             send(
                 zed_out.at[j, (z + d) % 4], zed_in.at[j, d - 1],
@@ -170,31 +183,33 @@
     def combine(j, copies, scale):
         for copy in copies:
             copy.wait_recv()
-        total = part[j % 2, z, k]
+        total = part[j, z]
         for d in range(3):
             total = total + zed_in[j, d].astype(F32)
         pooled = (total * scale).astype(BF)
-        rows = pl.ds(j * W, W)
-        term = dot(feats[j, y, x], w_self[rows, :]) + dot(pooled, w_neigh[rows, :])
-        pre[...] = term if j == 0 else pre[...] + term
-
-    sends = []
+        pre[...] += dot(pooled, w_neigh[pl.ds(j * W, W), :])
+
     encode(0)
     pl.semaphore_wait(barrier, 13)
-    first, second = [gather1(0)], []
+    first, second, third = [gather1(0)], [], []
     for j in range(1, NC):
         encode(j)
         first.append(gather1(j))
         second.append(gather2(j - 1, first[j - 1]))
+    third.append(gather3(0, second[0]))
     rest[0].wait()
+    lax.fori_loop(0, 4, adjacency, 0)
     second.append(gather2(NC - 1, first[NC - 1]))
-    lax.fori_loop(0, 8, adjacency, 0)
+    third.append(gather3(1, second[1]))
+    lax.fori_loop(4, 8, adjacency, 0)
     deg_copies = [
         send(
             deg_out.at[(c + d) % 8], deg_in.at[d - 1], deg_s.at[d - 1], deg_r.at[d - 1], at_col(d)
         )
         for d in range(1, 8)
     ]
+    third.append(gather3(2, second[2]))
+    core, zed = [aggregate(0, third[0])], []
 
     def flip(m, _):
         def pair(n, _):
@@ -207,8 +222,15 @@
         lax.fori_loop(0, m + 1, pair, 0)
         return 0
 
-    lax.fori_loop(0, 8, flip, 0)
-
+    lax.fori_loop(0, 6, flip, 0)
+    zed.append(column_sum(0, core[0]))
+    core.append(aggregate(1, third[1]))
+    third.append(gather3(3, second[3]))
+    zed.append(column_sum(1, core[1]))
+    for copy in rest[1:]:
+        copy.wait()
+    own = jnp.concatenate([feats[j, y, x] for j in range(NC)], axis=1)
+    pre[...] = dot(own, w_self[...])
     for copy in deg_copies:
         copy.wait_recv()
     degree = deg_out[c]
@@ -216,16 +238,15 @@
         degree = degree + deg_in[d]
     inv_row = lax.rsqrt(1.0 + degree)[0:1, :]
     inv_column = jnp.broadcast_to(inv_row, (128, 128)).T[:, 0:1]
-
-    for copy in rest[1:]:
-        copy.wait()
-    core, zed = [], []
-    for j in range(NC):
-        core.append(aggregate(j, second[j]))
-        zed.append(column_sum(j, core[j]))
-        if j >= 1:
-            combine(j - 1, zed[j - 1], inv_column)
-    combine(NC - 1, zed[NC - 1], inv_column)
+    combine(0, zed[0], inv_column)
+    core.append(aggregate(2, third[2]))
+    lax.fori_loop(6, 8, flip, 0)
+    zed.append(column_sum(2, core[2]))
+    combine(1, zed[1], inv_column)
+    core.append(aggregate(3, third[3]))
+    combine(2, zed[2], inv_column)
+    zed.append(column_sum(3, core[3]))
+    combine(3, zed[3], inv_column)
 
     v = pre[...]
     sg = 1.0 / (1.0 + jnp.exp(-v))
@@ -233,18 +254,21 @@
     dpre = (out_grad[...].astype(F32) * sg * (1.0 + v * (1.0 - sg))).astype(BF)
 
     around = []
-    for j in range(NC):
-        rows = pl.ds(j * W, W)
-        dagg[j, c] = (dot_nt(w_neigh[rows, :], dpre) * inv_row).astype(BF)
+
+    def spread(j):
+        dagg[j, c] = (dot_nt(w_neigh[pl.ds(j * W, W), :], dpre) * inv_row).astype(BF)
         own = dagg.at[j, c]
         around.append(
             [send(own, own, dg_s.at[j, d - 1], dg_r.at[j, d - 1], at_z(d)) for d in STEPS]
             + [send(own, own, dg_s.at[j, 3], dg_r.at[j, 3], sibling)]
         )
+
+    spread(0)
+    spread(1)
     for j in range(NC):
         dself[j] = dot_nt(w_self[pl.ds(j * W, W), :], dpre)
 
-    for copies in first + second + zed:
+    for copies in first + second + third + zed:
         for copy in copies:
             copy.wait_send()
     for copy in core + deg_copies:
@@ -260,35 +284,59 @@
             out.append(send(block, block, fw_s.at[j, d - 1], fw_r.at[j, d - 1], sibling))
         return out
 
-    def scatter1(j, passed):
+    def transpose_product(j, passed):
         around[j][3].wait_recv()
         for copy in passed:
             copy.wait_recv()
         chunk = jnp.concatenate([dagg[j, q] for q in range(8)], axis=1)
-
-        def tile(n, _):
-            p = dot(chunk, adj[:, pl.ds(pl.multiple_of(n * 256, 256), 256)]).astype(BF)
-            for i in range(2):
-                block = p[:, i * 128 : (i + 1) * 128]
-                yy, xx = n // 2, (n % 2) * 2 + i
-                feats[j, yy, xx, :, 0:128] = block[0:128]
-                feats[j, yy, xx, :, 128:256] = block[128:256]
-            return 0
-
-        lax.fori_loop(0, 8, tile, 0)
+        p = dot(chunk, adj[...]).astype(BF)
+        for i in range(16):
+            feats[j, i // 4, i % 4, :, 0:128] = p[0:128, i * 128 : (i + 1) * 128]
+            feats[j, i // 4, i % 4, :, 128:256] = p[128:256, i * 128 : (i + 1) * 128]
+
+    LOWER, UPPER = pl.ds(0, 2), pl.ds(2, 2)
+    WAYS = ((1, LOWER, UPPER), (3, UPPER, LOWER))
+
+    def scatter1(j):
+        relayed, direct = [], []
+        for n, (d, via, straight) in enumerate(WAYS):
+            far = (y + 2) % 4, (x + 2) % 4
+            near = (y + d) % 4, (x + d) % 4
+            a, b = feats.at[j, far[0], via, :, A], feats.at[j, via, far[1], :, B]
+            into = pl.ds(2 * n, 2)
+            relayed.append(
+                send(a, hop1_in.at[j, 0, 2, into], h1_s.at[j, n], h1_r.at[j, n], at_y(d))
+            )
+            relayed.append(
+                send(b, hop1_in.at[j, 1, 2, into], h1_s.at[j, 2 + n], h1_r.at[j, 2 + n], at_x(d))
+            )
+            a, b = feats.at[j, near[0], straight, :, A], feats.at[j, straight, near[1], :, B]
+            direct.append(
+                send(a, hop1_in.at[j, 0, n, straight], h1_s.at[j, 4 + n], h1_r.at[j, 4 + n], at_y(d))
+            )
+            direct.append(
+                send(b, hop1_in.at[j, 1, n, straight], h1_s.at[j, 6 + n], h1_r.at[j, 6 + n], at_x(d))
+            )
+        return relayed, direct
+
+    def relay(j, relayed):
         out = []
-        for d in STEPS:
+        for n, (d, via, _) in enumerate(WAYS):
+            relayed[2 * n].wait_recv()
+            relayed[2 * n + 1].wait_recv()
+            near_y, near_x = (y + d) % 4, (x + d) % 4
+            for q in range(2):
+                i = 2 * n + q
+                a = feats[j, near_y, i, :, 0:128].astype(F32) + hop1_in[j, 0, 2, i].astype(F32)
+                b = feats[j, i, near_x, :, 128:256].astype(F32) + hop1_in[j, 1, 2, i].astype(F32)
+                feats[j, near_y, i, :, 0:128] = a.astype(BF)
+                feats[j, i, near_x, :, 128:256] = b.astype(BF)
+            a, b = feats.at[j, near_y, via, :, A], feats.at[j, via, near_x, :, B]
             out.append(
-                send(
-                    feats.at[j, (y + d) % 4, :, :, A], hop1_in.at[j, 0, d - 1],
-                    h1_s.at[j, d - 1], h1_r.at[j, d - 1], at_y(d),
-                )
+                send(a, hop1_in.at[j, 0, n, via], h1_s.at[j, 8 + n], h1_r.at[j, 8 + n], at_y(d))
             )
             out.append(
-                send(
-                    feats.at[j, :, (x + d) % 4, :, B], hop1_in.at[j, 1, d - 1],
-                    h1_s.at[j, 2 + d], h1_r.at[j, 2 + d], at_x(d),
-                )
+                send(b, hop1_in.at[j, 1, n, via], h1_s.at[j, 10 + n], h1_r.at[j, 10 + n], at_x(d))
             )
         return out
 
@@ -298,15 +346,15 @@
         for q in range(4):
             a = feats[j, y, q, :, 0:128].astype(F32)
             b = feats[j, q, x, :, 128:256].astype(F32)
-            for d in range(3):
-                a = a + hop1_in[j, 0, d, q].astype(F32)
-                b = b + hop1_in[j, 1, d, q].astype(F32)
-            part[0, q, 0, :, 0:128] = a
-            part[0, q, 0, :, 128:256] = b
+            for n in range(2):
+                a = a + hop1_in[j, 0, n, q].astype(F32)
+                b = b + hop1_in[j, 1, n, q].astype(F32)
+            part[0, q, :, 0:128] = a
+            part[0, q, :, 128:256] = b
             core_out[j, q, :, 0:128] = a.astype(BF)
             core_out[j, q, :, 128:256] = b.astype(BF)
-        keep[j, 0] = part[0, x, 0, :, 0:128]
-        keep[j, 1] = part[0, y, 0, :, 128:256]
+        keep[j, 0] = part[0, x, :, 0:128]
+        keep[j, 1] = part[0, y, :, 128:256]
         out = []
         for d in STEPS:
             out.append(
@@ -333,32 +381,36 @@
                 total = total + hop2_in[j, h, d].astype(F32)
             halves.append(total)
         dx0 = jnp.concatenate(halves, axis=0) + dself[j]
-        part[1, 0, 0] = dx0.T * (1.0 / 16.0)
+        part[1, 0] = dx0.T * (1.0 / 16.0)
 
         def tile(m, _):
             rows = pl.ds(m * 256, 256)
             s = squash[j, rows, :].reshape(16, 16, W)
-            g = part[1, 0, 0, pl.ds(m * 16, 16), :].reshape(16, 1, W)
+            g = part[1, 0, pl.ds(m * 16, 16), :].reshape(16, 1, W)
             dzeta[rows, :] = (g * (1.0 - s * s)).astype(BF).reshape(256, W)
             return 0
 
         lax.fori_loop(0, 8, tile, 0)
 
         def term(m, _):
-            rows = pl.ds(m * 256, 256)
+            rows = pl.ds(m * 1024, 1024)
             squash[j, rows, :] = dot(states[rows, :], dzeta[...])
-            for g in range(8):
-                away = squash[j, pl.ds(m * 256 + g * 32 + other * 16, 16), :].astype(BF)
-                enc[j, pl.ds(m * 128 + g * 16, 16), :] = away
+            for g in range(32):
+                away = squash[j, pl.ds(m * 1024 + g * 32 + other * 16, 16), :].astype(BF)
+                enc[j, pl.ds(m * 512 + g * 16, 16), :] = away
+            raw_half(j, m).start()
             return 0
 
-        lax.fori_loop(0, 8, term, 0)
-        return send(
-            enc.at[j, pl.ds(0, 1024)], rcore_in.at[j], rc_s.at[j], rc_r.at[j], sibling
+        lax.fori_loop(0, 2, term, 0)
+
+    def raw_half(j, m):
+        rows = pl.ds(m * 512, 512)
+        return describe(
+            enc.at[j, rows], rcore_in.at[j, rows], rc_s.at[j, m], rc_r.at[j, m], sibling
         )
 
-    def term_zed(j, copy):
-        copy.wait_recv()
+    def term_zed(j, half):
+        raw_half(j, half).wait_recv()
 
         def tile(m, _):
             for q in range(4):
@@ -369,11 +421,13 @@
                 enc[j, pl.ds(1024 + q * 256 + m * 16, 16), :] = total.astype(BF)
             return 0
 
-        lax.fori_loop(0, 16, tile, 0)
+        lax.fori_loop(half * 8, half * 8 + 8, tile, 0)
+        into = pl.ds(half * 128, 128)
         return [
             send(
-                enc.at[j, pl.ds(1024 + ((z + d) % 4) * 256, 256)], rzed_in.at[j, d - 1],
-                rz_s.at[j, d - 1], rz_r.at[j, d - 1], at_z(d),
+                enc.at[j, pl.ds(1024 + ((z + d) % 4) * 256 + half * 128, 128)],
+                rzed_in.at[j, d - 1, into],
+                rz_s.at[j, half * 3 + d - 1], rz_r.at[j, half * 3 + d - 1], at_z(d),
             )
             for d in STEPS
         ]
@@ -388,12 +442,13 @@
                 total = total + rzed_in[j, d, pl.ds(m * 16, 16), :].astype(F32)
             rx_out = pl.ds((m % 4) * 64 + (m // 4) * 16, 16)
             sums[j, rx_out, :] = total
+            sums_out[j, rx_out, :] = total.astype(BF)
             return 0
 
         lax.fori_loop(0, 16, tile, 0)
         return [
             send(
-                sums.at[j, pl.ds(((x + d) % 4) * 64, 64)], rx_in.at[j, d - 1],
+                sums_out.at[j, pl.ds(((x + d) % 4) * 64, 64)], rx_in.at[j, d - 1],
                 rx_s.at[j, d - 1], rx_r.at[j, d - 1], at_x(d),
             )
             for d in STEPS
@@ -404,7 +459,7 @@
             copy.wait_recv()
         total = sums[j, pl.ds(x * 64, 64), :]
         for d in range(3):
-            total = total + rx_in[j, d]
+            total = total + rx_in[j, d].astype(F32)
         last[j] = total
         return [
             send(
@@ -424,39 +479,54 @@
             total = total + ry_in[j, d]
         enc_grad[:, j * W : (j + 1) * W] = total * factor
 
-    passed, hop1, hop2 = [forward(0)], [], []
-    for j in range(NC - 1):
-        passed.append(forward(j + 1))
-        hop1.append(scatter1(j, passed[j]))
-    hop2.append(scatter2(0, hop1[0]))
-    hop1.append(scatter1(NC - 1, passed[NC - 1]))
-    rcore, rzed, rx, ry = [], [], [], []
+    passed, relayed, direct, hop1 = [], [], [], []
+    hop2, rzed, rx, ry = [], [], [], []
+
+    def product(j):
+        passed.append(forward(j))
+        if j + 2 < NC:
+            spread(j + 2)
+        transpose_product(j, passed[j])
+
+    def first_hop(j):
+        for kept, copies in zip((relayed, direct), scatter1(j)):
+            kept.append(copies)
+
+    def pass_on(j):
+        hop1.append(relay(j, relayed[j]))
+
+    def second_hop(j):
+        hop2.append(scatter2(j, direct[j] + hop1[j]))
+
+    def raw(j):
+        encoder_term(j, hop2[j])
+
+    def raw_z(j):
+        rzed.append(term_zed(j, 0) + term_zed(j, 1))
+
+    def raw_x(j):
+        rx.append(term_x(j, rzed[j]))
+
+    def raw_y(j):
+        ry.append(term_y(j, rx[j]))
+
+    for step, j in (
+        (product, 0), (first_hop, 0), (product, 1), (pass_on, 0), (first_hop, 1), (product, 2),
+        (second_hop, 0), (pass_on, 1), (first_hop, 2), (raw, 0), (second_hop, 1), (pass_on, 2),
+        (product, 3), (first_hop, 3), (raw_z, 0), (raw, 1), (second_hop, 2), (pass_on, 3),
+        (raw_z, 1), (raw_x, 0), (raw, 2), (second_hop, 3), (raw_z, 2), (raw_y, 0), (raw_x, 1),
+        (raw, 3), (raw_y, 1), (raw_x, 2), (raw_z, 3), (raw_y, 2), (raw_x, 3), (raw_y, 3),
+    ):
+        step(j)
     for j in range(NC):
-        rcore.append(encoder_term(j, hop2[j]))
-        if j + 1 < NC:
-            hop2.append(scatter2(j + 1, hop1[j + 1]))
-        if j >= 1:
-            rzed.append(term_zed(j - 1, rcore[j - 1]))
-        if j >= 2:
-            rx.append(term_x(j - 2, rzed[j - 2]))
-        if j >= 3:
-            ry.append(term_y(j - 3, rx[j - 3]))
-    rzed.append(term_zed(NC - 1, rcore[NC - 1]))
-    rx.append(term_x(NC - 2, rzed[NC - 2]))
-    ry.append(term_y(NC - 3, rx[NC - 3]))
-    finish(0, ry[0])
-    rx.append(term_x(NC - 1, rzed[NC - 1]))
-    ry.append(term_y(NC - 2, rx[NC - 2]))
-    finish(1, ry[1])
-    ry.append(term_y(NC - 1, rx[NC - 1]))
-    finish(2, ry[2])
-    finish(3, ry[3])
-
-    for copies in around + passed + hop1 + hop2 + rzed + rx + ry:
+        finish(j, ry[j])
+
+    for copies in around + passed + relayed + direct + hop1 + hop2 + rzed + rx + ry:
         for copy in copies:
             copy.wait_send()
-    for copy in rcore:
-        copy.wait_send()
+    for j in range(NC):
+        for half in range(2):
+            raw_half(j, half).wait_send()
 
 
 def local(
@@ -479,7 +549,7 @@
         V((1024, 2048), BF),
         V((NC, 2048, W), F32),
         V((NC, 4, 4, 128, W), BF),
-        V((2, 4, 2, 128, W), F32),
+        V((NC, 4, 128, W), F32),
         V((128, 1024), BF),
         V((NC, 4, 128, W), BF),
         V((NC, 4, 128, W), BF),
@@ -496,13 +566,14 @@
         V((2048, W), BF),
         V((NC, 1024, W), BF),
         V((NC, 3, 256, W), BF),
-        V((NC, 3, 64, W), F32),
+        V((NC, 3, 64, W), BF),
         V((NC, 3, 16, W), F32),
         V((NC, 256, W), F32),
+        V((NC, 256, W), BF),
         V((NC, 64, W), F32),
     ]
     shapes = [
-        (NC, 12), (7,), (NC,), (NC, 3), (NC, 4), (NC, 3), (NC, 6), (NC, 6), (NC,), (NC, 3),
+        (NC, 14), (7,), (NC,), (NC, 3), (NC, 4), (NC, 3), (NC, 12), (NC, 6), (NC, 2), (NC, 6),
         (NC, 3), (NC, 3),
     ]
     semaphores = [S((16,))] + [S(shape) for shape in shapes for _ in range(2)]

time: 156 us -> 129 us (0.83)
  Pallas kernels: 151 us -> 124 us
    pallas_call x1, Pallas kernels: 151 us -> 124 us  [local(): pl.pallas_call(kernel, out_shape=(jax.ShapeDtypeStruct((128, 1024), BF),...]
where the time goes in v2:
time: 129 us
  Pallas kernels  124 us (96%)
  local copies, waits for them, and re-layouts  3.14 us (2%)
  between operations  1.29 us (1%)
    pallas_call x1, Pallas kernels, local(): pl.pallas_call(kernel, out_shape=(jax.ShapeDtypeStruct((128, 1024), BF),...  124 us
    unnamed x2, local copies, waits for them, and re-layouts  3.14 us

profile of v2, /device:TPU:0, one launch (start us, length us, event | category | flops | bytes accessed | tf_op | source)
XLA Modules:
  0.0 128.6 jit_solution(2027034327388707889)
XLA Ops:
  1.3 124.2 %step.1 = (bf16[128,1024]{1,0:T(8,128)(2,1)}, f32[16,1024]{1,0:T(8,128)}) custom-call(bf16[2048,2048]{1,0:T(8,128)(2,1)} %bitcast.3, bf16[2048,1024]{1,0:T(8,128)(2,1)} %enc_h.1, bf16[1024,1024]{1,0:T(8,128)(2,1)} %self_h.1, bf16[1024,1024]{1,0:T(8,128)(2,1)} %neigh_h.1, bf16[1024,16,128]{2,1,0:T(8,128)(2,1)} %bitcast.4, bf16[128,1024]{1,0:T(8,128)(2,1)} %grad_h.1, ...), custom_call_target="tpu_custom_call" | custom-call | tf_op jit(solution)/shard_map/step/pallas_call | solution.py:580
  125.5 1.7 %copy.13 = bf16[128,1024]{1,0:T(8,128)(2,1)} copy(bf16[128,1024]{1,0:T(8,128)(2,1)} %get-tuple-element.4) | data formatting | bytes 524288
  127.1 1.5 %copy.14 = f32[16,1024]{1,0:T(8,128)} copy(f32[16,1024]{1,0:T(8,128)} %get-tuple-element.5) | data formatting | bytes 131072

commit v3 on v2

--- a/solution.py
+++ b/solution.py
@@ -64,26 +64,20 @@
         return copy
 
     def load_states(m):
-        rows = pl.ds(m * 256, 256)
+        rows = pl.ds(m * 512, 512)
         return pltpu.make_async_copy(states_h.at[rows], states.at[rows], load_sem.at[m])
 
     def load_enc(j):
         return pltpu.make_async_copy(enc_h.at[:, pl.ds(j * W, W)], enc.at[j], load_sem.at[8 + j])
 
     load_enc(0).start()
-    for m in range(8):
-        load_states(m).start()
-    for j in range(1, NC):
-        load_enc(j).start()
+    load_states(0).start()
     rest = [
         pltpu.make_async_copy(src, dst, load_sem.at[12 + n])
         for n, (src, dst) in enumerate(
             [(edge_h, edge), (self_h, w_self), (neigh_h, w_neigh), (grad_h, out_grad)]
         )
     ]
-    for copy in rest:
-        copy.start()
-
     barrier = pltpu.get_barrier_semaphore()
     for d in STEPS:
         pl.semaphore_signal(barrier, inc=1, device_id=at_x(d), device_id_type=MESH)
@@ -93,14 +87,23 @@
 
     def encode(j):
         load_enc(j).wait()
-
+        if j == 0:
+            load_states(1).start()
         size = 512 if j == 0 else 1024
 
         def tile(m, _):
             rows = pl.ds(m * size, size)
             if j == 0:
-                load_states(2 * m).wait()
-                load_states(2 * m + 1).wait()
+                load_states(m).wait()
+
+                @pl.when(m < 2)
+                def _():
+                    load_states(m + 2).start()
+
+                @pl.when(m == 2)
+                def _():
+                    load_enc(1).start()
+
             s = jnp.tanh(dot(states[rows, :], enc[j]))
             squash[j, rows, :] = s
             mean = jnp.sum(s.reshape(size // 16, 16, W), axis=1) * (1.0 / 16.0)
@@ -164,14 +167,18 @@
             copy.wait_recv()
         p = dot(adj[...], feats[j].reshape(2048, W)).reshape(4, 2, 128, W)
         part[j] = jnp.where(k == 0, p[:, 0], p[:, 1])
-        core_out[j] = jnp.where(k == 0, p[:, 1], p[:, 0]).astype(BF)
+        away = jnp.where(k == 0, p[:, 1], p[:, 0]).astype(BF)
+        core_out[j, :, 0] = away[:, :, 0:128]
+        core_out[j, :, 1] = away[:, :, 128:256]
         return send(core_out.at[j], core_in.at[j], core_s.at[j], core_r.at[j], sibling)
 
     def column_sum(j, copy):
         copy.wait_recv()
         for q in range(4):
-            part[j, q] = part[j, q] + core_in[j, q].astype(F32)
-            zed_out[j, q] = part[j, q].astype(BF)
+            came = jnp.concatenate([core_in[j, q, 0], core_in[j, q, 1]], axis=1)
+            total = part[j, q] + came.astype(F32)
+            part[j, q] = total
+            zed_out[j, q] = total.astype(BF)
         return [
             send(
                 zed_out.at[j, (z + d) % 4], zed_in.at[j, d - 1],
@@ -192,6 +199,10 @@
     encode(0)
     pl.semaphore_wait(barrier, 13)
     first, second, third = [gather1(0)], [], []
+    for j in range(2, NC):
+        load_enc(j).start()
+    for copy in rest:
+        copy.start()
     for j in range(1, NC):
         encode(j)
         first.append(gather1(j))
@@ -208,9 +219,6 @@
         )
         for d in range(1, 8)
     ]
-    third.append(gather3(2, second[2]))
-    core, zed = [aggregate(0, third[0])], []
-
     def flip(m, _):
         def pair(n, _):
             a, b = pl.ds(m * 256, 256), pl.ds(n * 256, 256)
@@ -222,10 +230,12 @@
         lax.fori_loop(0, m + 1, pair, 0)
         return 0
 
-    lax.fori_loop(0, 6, flip, 0)
+    core, zed = [aggregate(0, third[0])], []
+    third.append(gather3(2, second[2]))
+    third.append(gather3(3, second[3]))
+    core.append(aggregate(1, third[1]))
     zed.append(column_sum(0, core[0]))
-    core.append(aggregate(1, third[1]))
-    third.append(gather3(3, second[3]))
+    core.append(aggregate(2, third[2]))
     zed.append(column_sum(1, core[1]))
     for copy in rest[1:]:
         copy.wait()
@@ -239,13 +249,13 @@
     inv_row = lax.rsqrt(1.0 + degree)[0:1, :]
     inv_column = jnp.broadcast_to(inv_row, (128, 128)).T[:, 0:1]
     combine(0, zed[0], inv_column)
-    core.append(aggregate(2, third[2]))
-    lax.fori_loop(6, 8, flip, 0)
+    core.append(aggregate(3, third[3]))
     zed.append(column_sum(2, core[2]))
     combine(1, zed[1], inv_column)
-    core.append(aggregate(3, third[3]))
+    lax.fori_loop(0, 3, flip, 0)
+    zed.append(column_sum(3, core[3]))
     combine(2, zed[2], inv_column)
-    zed.append(column_sum(3, core[3]))
+    lax.fori_loop(3, 6, flip, 0)
     combine(3, zed[3], inv_column)
 
     v = pre[...]
@@ -264,17 +274,15 @@
         )
 
     spread(0)
-    spread(1)
     for j in range(NC):
         dself[j] = dot_nt(w_self[pl.ds(j * W, W), :], dpre)
+    lax.fori_loop(6, 8, flip, 0)
 
     for copies in first + second + third + zed:
         for copy in copies:
             copy.wait_send()
     for copy in core + deg_copies:
         copy.wait_send()
-
-    A, B = pl.ds(0, 128), pl.ds(128, 128)
 
     def forward(j):
         out = []
@@ -284,6 +292,9 @@
             out.append(send(block, block, fw_s.at[j, d - 1], fw_r.at[j, d - 1], sibling))
         return out
 
+    def piece(j, half, major, minor, blocks):
+        return pl.ds(((j * 2 + half) * 16 + major * 4 + minor) * 8, blocks * 8)
+
     def transpose_product(j, passed):
         around[j][3].wait_recv()
         for copy in passed:
@@ -291,81 +302,76 @@
         chunk = jnp.concatenate([dagg[j, q] for q in range(8)], axis=1)
         p = dot(chunk, adj[...]).astype(BF)
         for i in range(16):
-            feats[j, i // 4, i % 4, :, 0:128] = p[0:128, i * 128 : (i + 1) * 128]
-            feats[j, i // 4, i % 4, :, 128:256] = p[128:256, i * 128 : (i + 1) * 128]
-
-    LOWER, UPPER = pl.ds(0, 2), pl.ds(2, 2)
-    WAYS = ((1, LOWER, UPPER), (3, UPPER, LOWER))
+            yy, xx, lanes = i // 4, i % 4, slice(i * 128, (i + 1) * 128)
+            edge[piece(j, 0, yy, xx, 1)] = p[0:128, lanes].reshape(8, 16, 128)
+            edge[piece(j, 1, xx, yy, 1)] = p[128:256, lanes].reshape(8, 16, 128)
+
+    WAYS = ((1, 0, 2), (3, 2, 0))
 
     def scatter1(j):
         relayed, direct = [], []
         for n, (d, via, straight) in enumerate(WAYS):
-            far = (y + 2) % 4, (x + 2) % 4
-            near = (y + d) % 4, (x + d) % 4
-            a, b = feats.at[j, far[0], via, :, A], feats.at[j, via, far[1], :, B]
-            into = pl.ds(2 * n, 2)
-            relayed.append(
-                send(a, hop1_in.at[j, 0, 2, into], h1_s.at[j, n], h1_r.at[j, n], at_y(d))
-            )
-            relayed.append(
-                send(b, hop1_in.at[j, 1, 2, into], h1_s.at[j, 2 + n], h1_r.at[j, 2 + n], at_x(d))
-            )
-            a, b = feats.at[j, near[0], straight, :, A], feats.at[j, straight, near[1], :, B]
-            direct.append(
-                send(a, hop1_in.at[j, 0, n, straight], h1_s.at[j, 4 + n], h1_r.at[j, 4 + n], at_y(d))
-            )
-            direct.append(
-                send(b, hop1_in.at[j, 1, n, straight], h1_s.at[j, 6 + n], h1_r.at[j, 6 + n], at_x(d))
-            )
+            into = pl.ds(2 * n * 8, 16)
+            for half, at, place in ((0, at_y, y), (1, at_x, x)):
+                relayed.append(
+                    send(
+                        edge.at[piece(j, half, (place + 2) % 4, via, 2)],
+                        hop1_in.at[j, half, 2, into],
+                        h1_s.at[j, 2 * n + half], h1_r.at[j, 2 * n + half], at(d),
+                    )
+                )
+        for n, (d, via, straight) in enumerate(WAYS):
+            into = pl.ds(straight * 8, 16)
+            for half, at, place in ((0, at_y, y), (1, at_x, x)):
+                direct.append(
+                    send(
+                        edge.at[piece(j, half, (place + d) % 4, straight, 2)],
+                        hop1_in.at[j, half, n, into],
+                        h1_s.at[j, 4 + 2 * n + half], h1_r.at[j, 4 + 2 * n + half], at(d),
+                    )
+                )
         return relayed, direct
 
     def relay(j, relayed):
         out = []
         for n, (d, via, _) in enumerate(WAYS):
-            relayed[2 * n].wait_recv()
-            relayed[2 * n + 1].wait_recv()
-            near_y, near_x = (y + d) % 4, (x + d) % 4
-            for q in range(2):
-                i = 2 * n + q
-                a = feats[j, near_y, i, :, 0:128].astype(F32) + hop1_in[j, 0, 2, i].astype(F32)
-                b = feats[j, i, near_x, :, 128:256].astype(F32) + hop1_in[j, 1, 2, i].astype(F32)
-                feats[j, near_y, i, :, 0:128] = a.astype(BF)
-                feats[j, i, near_x, :, 128:256] = b.astype(BF)
-            a, b = feats.at[j, near_y, via, :, A], feats.at[j, via, near_x, :, B]
-            out.append(
-                send(a, hop1_in.at[j, 0, n, via], h1_s.at[j, 8 + n], h1_r.at[j, 8 + n], at_y(d))
-            )
-            out.append(
-                send(b, hop1_in.at[j, 1, n, via], h1_s.at[j, 10 + n], h1_r.at[j, 10 + n], at_x(d))
-            )
+            for half, at, place in ((0, at_y, y), (1, at_x, x)):
+                relayed[2 * n + half].wait_recv()
+                mine = piece(j, half, (place + d) % 4, via, 2)
+                came = hop1_in[j, half, 2, pl.ds(2 * n * 8, 16)].astype(F32)
+                edge[mine] = (edge[mine].astype(F32) + came).astype(BF)
+                out.append(
+                    send(
+                        edge.at[mine], hop1_in.at[j, half, n, pl.ds(via * 8, 16)],
+                        h1_s.at[j, 8 + 2 * n + half], h1_r.at[j, 8 + 2 * n + half], at(d),
+                    )
+                )
         return out
 
     def scatter2(j, copies):
         for copy in copies:
             copy.wait_recv()
         for q in range(4):
-            a = feats[j, y, q, :, 0:128].astype(F32)
-            b = feats[j, q, x, :, 128:256].astype(F32)
-            for n in range(2):
-                a = a + hop1_in[j, 0, n, q].astype(F32)
-                b = b + hop1_in[j, 1, n, q].astype(F32)
-            part[0, q, :, 0:128] = a
-            part[0, q, :, 128:256] = b
-            core_out[j, q, :, 0:128] = a.astype(BF)
-            core_out[j, q, :, 128:256] = b.astype(BF)
+            for half, place in ((0, y), (1, x)):
+                total = edge[piece(j, half, place, q, 1)].astype(F32)
+                for n in range(2):
+                    total = total + hop1_in[j, half, n, pl.ds(q * 8, 8)].astype(F32)
+                total = total.reshape(128, 128)
+                part[0, q, :, half * 128 : half * 128 + 128] = total
+                core_out[j, q, half] = total.astype(BF)
         keep[j, 0] = part[0, x, :, 0:128]
         keep[j, 1] = part[0, y, :, 128:256]
         out = []
         for d in STEPS:
             out.append(
                 send(
-                    core_out.at[j, (x + d) % 4, :, A], hop2_in.at[j, 0, d - 1],
+                    core_out.at[j, (x + d) % 4, 0], hop2_in.at[j, 0, d - 1],
                     h2_s.at[j, d - 1], h2_r.at[j, d - 1], at_x(d),
                 )
             )
             out.append(
                 send(
-                    core_out.at[j, (y + d) % 4, :, B], hop2_in.at[j, 1, d - 1],
+                    core_out.at[j, (y + d) % 4, 1], hop2_in.at[j, 1, d - 1],
                     h2_s.at[j, 2 + d], h2_r.at[j, 2 + d], at_y(d),
                 )
             )
@@ -411,6 +417,7 @@
 
     def term_zed(j, half):
         raw_half(j, half).wait_recv()
+        base = 1024 + half * 512
 
         def tile(m, _):
             for q in range(4):
@@ -418,38 +425,51 @@
                 mine = pl.ds(g * 32 + k * 16, 16)
                 total = squash[j, mine, :] + rcore_in[j, pl.ds(g * 16, 16), :].astype(F32)
                 squash[j, mine, :] = total
-                enc[j, pl.ds(1024 + q * 256 + m * 16, 16), :] = total.astype(BF)
+                if half == 0:
+                    slot = q * 128 + m * 16
+                else:
+                    slot = (m % 4) * 128 + ((m // 4 - 2) * 4 + q) * 16
+                enc[j, pl.ds(base + slot, 16), :] = total.astype(BF)
             return 0
 
         lax.fori_loop(half * 8, half * 8 + 8, tile, 0)
+        place, at = ((z, at_z), (x, at_x))[half]
         into = pl.ds(half * 128, 128)
         return [
             send(
-                enc.at[j, pl.ds(1024 + ((z + d) % 4) * 256 + half * 128, 128)],
+                enc.at[j, pl.ds(base + ((place + d) % 4) * 128, 128)],
                 rzed_in.at[j, d - 1, into],
-                rz_s.at[j, half * 3 + d - 1], rz_r.at[j, half * 3 + d - 1], at_z(d),
+                rz_s.at[j, half * 3 + d - 1], rz_r.at[j, half * 3 + d - 1], at(d),
             )
             for d in STEPS
         ]
 
-    def term_x(j, copies):
+    def term_x(j, half, copies):
         for copy in copies:
             copy.wait_recv()
 
         def tile(m, _):
-            total = squash[j, pl.ds((m * 4 + z) * 32 + k * 16, 16), :]
+            if half == 0:
+                row = (m * 4 + z) * 32
+                slot = (m % 4) * 32 + (m // 4) * 16
+            else:
+                row = (((2 + m // 4) * 4 + x) * 4 + m % 4) * 32
+                slot = 128 + (m % 4) * 32 + (m // 4) * 16
+            total = squash[j, pl.ds(row + k * 16, 16), :]
             for d in range(3):
-                total = total + rzed_in[j, d, pl.ds(m * 16, 16), :].astype(F32)
-            rx_out = pl.ds((m % 4) * 64 + (m // 4) * 16, 16)
-            sums[j, rx_out, :] = total
-            sums_out[j, rx_out, :] = total.astype(BF)
+                came = rzed_in[j, d, pl.ds(half * 128 + m * 16, 16), :]
+                total = total + came.astype(F32)
+            sums[j, pl.ds(slot, 16), :] = total
+            sums_out[j, pl.ds(slot, 16), :] = total.astype(BF)
             return 0
 
-        lax.fori_loop(0, 16, tile, 0)
+        lax.fori_loop(0, 8, tile, 0)
+        place, at = ((x, at_x), (z, at_z))[half]
         return [
             send(
-                sums_out.at[j, pl.ds(((x + d) % 4) * 64, 64)], rx_in.at[j, d - 1],
-                rx_s.at[j, d - 1], rx_r.at[j, d - 1], at_x(d),
+                sums_out.at[j, pl.ds(half * 128 + ((place + d) % 4) * 32, 32)],
+                rx_in.at[j, half, d - 1],
+                rx_s.at[j, half * 3 + d - 1], rx_r.at[j, half * 3 + d - 1], at(d),
             )
             for d in STEPS
         ]
@@ -457,10 +477,11 @@
     def term_y(j, copies):
         for copy in copies:
             copy.wait_recv()
-        total = sums[j, pl.ds(x * 64, 64), :]
-        for d in range(3):
-            total = total + rx_in[j, d].astype(F32)
-        last[j] = total
+        for half, place in ((0, x), (1, z)):
+            total = sums[j, pl.ds(half * 128 + place * 32, 32), :]
+            for d in range(3):
+                total = total + rx_in[j, half, d].astype(F32)
+            last[j, half * 32 : half * 32 + 32, :] = total
         return [
             send(
                 last.at[j, pl.ds(((y + d) % 4) * 16, 16)], ry_in.at[j, d - 1],
@@ -484,8 +505,8 @@
 
     def product(j):
         passed.append(forward(j))
-        if j + 2 < NC:
-            spread(j + 2)
+        if j + 1 < NC:
+            spread(j + 1)
         transpose_product(j, passed[j])
 
     def first_hop(j):
@@ -505,17 +526,18 @@
         rzed.append(term_zed(j, 0) + term_zed(j, 1))
 
     def raw_x(j):
-        rx.append(term_x(j, rzed[j]))
+        rx.append(term_x(j, 0, rzed[j][:3]) + term_x(j, 1, rzed[j][3:]))
 
     def raw_y(j):
         ry.append(term_y(j, rx[j]))
 
     for step, j in (
         (product, 0), (first_hop, 0), (product, 1), (pass_on, 0), (first_hop, 1), (product, 2),
-        (second_hop, 0), (pass_on, 1), (first_hop, 2), (raw, 0), (second_hop, 1), (pass_on, 2),
-        (product, 3), (first_hop, 3), (raw_z, 0), (raw, 1), (second_hop, 2), (pass_on, 3),
-        (raw_z, 1), (raw_x, 0), (raw, 2), (second_hop, 3), (raw_z, 2), (raw_y, 0), (raw_x, 1),
-        (raw, 3), (raw_y, 1), (raw_x, 2), (raw_z, 3), (raw_y, 2), (raw_x, 3), (raw_y, 3),
+        (pass_on, 1), (second_hop, 0), (first_hop, 2), (product, 3), (first_hop, 3),
+        (second_hop, 1), (pass_on, 2), (raw, 0), (pass_on, 3), (second_hop, 2), (raw_z, 0),
+        (raw, 1), (second_hop, 3), (raw_z, 1), (raw_x, 0), (raw, 2), (raw_z, 2), (raw_x, 1),
+        (raw_y, 0), (raw, 3), (raw_x, 2), (raw_y, 1), (raw_z, 3), (raw_y, 2), (raw_x, 3),
+        (raw_y, 3),
     ):
         step(j)
     for j in range(NC):
@@ -527,6 +549,11 @@
     for j in range(NC):
         for half in range(2):
             raw_half(j, half).wait_send()
+
+
+def hand_over(a, b, a_out, b_out):
+    a_out[...] = a[...]
+    b_out[...] = b[...]
 
 
 def local(
@@ -551,8 +578,8 @@
         V((NC, 4, 4, 128, W), BF),
         V((NC, 4, 128, W), F32),
         V((128, 1024), BF),
-        V((NC, 4, 128, W), BF),
-        V((NC, 4, 128, W), BF),
+        V((NC, 4, 2, 128, 128), BF),
+        V((NC, 4, 2, 128, 128), BF),
         V((NC, 4, 128, W), BF),
         V((NC, 3, 128, W), BF),
         V((8, 8, 128), F32),
@@ -560,13 +587,13 @@
         V((128, 1024), F32),
         V((NC, 8, W, 128), BF),
         V((NC, W, 128), F32),
-        V((NC, 2, 3, 4, 128, 128), BF),
+        V((NC, 2, 3, 32, 16, 128), BF),
         V((NC, 2, 128, 128), F32),
         V((NC, 2, 3, 128, 128), BF),
         V((2048, W), BF),
         V((NC, 1024, W), BF),
         V((NC, 3, 256, W), BF),
-        V((NC, 3, 64, W), BF),
+        V((NC, 2, 3, 32, W), BF),
         V((NC, 3, 16, W), F32),
         V((NC, 256, W), F32),
         V((NC, 256, W), BF),
@@ -574,10 +601,10 @@
     ]
     shapes = [
         (NC, 14), (7,), (NC,), (NC, 3), (NC, 4), (NC, 3), (NC, 12), (NC, 6), (NC, 2), (NC, 6),
-        (NC, 3), (NC, 3),
+        (NC, 6), (NC, 3),
     ]
     semaphores = [S((16,))] + [S(shape) for shape in shapes for _ in range(2)]
-    return pl.pallas_call(
+    results = pl.pallas_call(
         kernel,
         out_shape=(
             jax.ShapeDtypeStruct((128, 1024), BF),
@@ -591,6 +618,13 @@
         ),
         name="step",
     )(states, enc_weight, self_weight, neighbour_weight, edge_weight, out_grad, tile_live, overflow)
+    return pl.pallas_call(
+        hand_over,
+        out_shape=tuple(jax.ShapeDtypeStruct(r.shape, r.dtype) for r in results),
+        in_specs=[vmem] * 2,
+        out_specs=(vmem,) * 2,
+        name="hand_over",
+    )(*results)
 
 
 def solution(mesh):

time: 129 us -> 125 us (0.969)
  local copies, waits for them, and re-layouts: 3.14 us -> 0 us
    unnamed x2 -> x0, local copies, waits for them, and re-layouts: 3.14 us -> none
    pallas_call x1, Pallas kernels: 124 us -> 122 us  [local(): pl.pallas_call(kernel, out_shape=(jax.ShapeDtypeStruct((128, 1024), BF),...]
    pallas_call x0 -> x1, Pallas kernels: none -> 1.69 us  [local(): pl.pallas_call(hand_over, out_shape=tuple((jax.ShapeDtypeStruct(r.shape,...]
where the time goes in v3:
time: 125 us
  Pallas kernels  124 us (99%)
  between operations  1.29 us (1%)
    pallas_call x1, Pallas kernels, local(): pl.pallas_call(kernel, out_shape=(jax.ShapeDtypeStruct((128, 1024), BF),...  122 us

profile of v3, /device:TPU:0, one launch (start us, length us, event | category | flops | bytes accessed | tf_op | source)
XLA Modules:
  0.0 124.9 jit_solution(8582210887616929948)
XLA Ops:
  1.3 121.9 %step.1 = (bf16[128,1024]{1,0:T(8,128)(2,1)}, f32[16,1024]{1,0:T(8,128)}) custom-call(bf16[2048,2048]{1,0:T(8,128)(2,1)} %bitcast.3, bf16[2048,1024]{1,0:T(8,128)(2,1)} %enc_h.1, bf16[1024,1024]{1,0:T(8,128)(2,1)} %self_h.1, bf16[1024,1024]{1,0:T(8,128)(2,1)} %neigh_h.1, bf16[1024,16,128]{2,1,0:T(8,128)(2,1)} %bitcast.4, bf16[128,1024]{1,0:T(8,128)(2,1)} %grad_h.1, ...), custom_call_target="tpu_custom_call" | custom-call | tf_op jit(solution)/shard_map/step/pallas_call | solution.py:607
  123.2 1.7 %hand_over.1 = (bf16[128,1024]{1,0:T(8,128)(2,1)}, f32[16,1024]{1,0:T(8,128)}) custom-call(bf16[128,1024]{1,0:T(8,128)(2,1)} %get-tuple-element.4.a, f32[16,1024]{1,0:T(8,128)} %get-tuple-element.5.b), custom_call_target="tpu_custom_call" | custom-call | tf_op jit(solution)/shard_map/hand_over/pallas_call | solution.py:621

commit v4 on v3

--- a/solution.py
+++ b/solution.py
@@ -277,6 +277,7 @@
     for j in range(NC):
         dself[j] = dot_nt(w_self[pl.ds(j * W, W), :], dpre)
     lax.fori_loop(6, 8, flip, 0)
+    spread(1)
 
     for copies in first + second + third + zed:
         for copy in copies:
@@ -505,8 +506,8 @@
 
     def product(j):
         passed.append(forward(j))
-        if j + 1 < NC:
-            spread(j + 1)
+        if j + 2 < NC:
+            spread(j + 2)
         transpose_product(j, passed[j])
 
     def first_hop(j):
@@ -532,12 +533,11 @@
         ry.append(term_y(j, rx[j]))
 
     for step, j in (
-        (product, 0), (first_hop, 0), (product, 1), (pass_on, 0), (first_hop, 1), (product, 2),
-        (pass_on, 1), (second_hop, 0), (first_hop, 2), (product, 3), (first_hop, 3),
-        (second_hop, 1), (pass_on, 2), (raw, 0), (pass_on, 3), (second_hop, 2), (raw_z, 0),
-        (raw, 1), (second_hop, 3), (raw_z, 1), (raw_x, 0), (raw, 2), (raw_z, 2), (raw_x, 1),
-        (raw_y, 0), (raw, 3), (raw_x, 2), (raw_y, 1), (raw_z, 3), (raw_y, 2), (raw_x, 3),
-        (raw_y, 3),
+        (product, 0), (first_hop, 0), (product, 1), (first_hop, 1), (pass_on, 0), (product, 2),
+        (first_hop, 2), (pass_on, 1), (product, 3), (first_hop, 3), (second_hop, 0), (pass_on, 2),
+        (second_hop, 1), (pass_on, 3), (raw, 0), (second_hop, 2), (second_hop, 3), (raw_z, 0),
+        (raw, 1), (raw_z, 1), (raw_x, 0), (raw, 2), (raw_z, 2), (raw_x, 1), (raw_y, 0), (raw, 3),
+        (raw_x, 2), (raw_y, 1), (raw_z, 3), (raw_y, 2), (raw_x, 3), (raw_y, 3),
     ):
         step(j)
     for j in range(NC):

time: 125 us -> 125 us (level)
  no operation moved by 1% of the time
where the time goes in v4:
time: 125 us
  Pallas kernels  124 us (99%)
  between operations  1.29 us (1%)
    pallas_call x1, Pallas kernels, local(): pl.pallas_call(kernel, out_shape=(jax.ShapeDtypeStruct((128, 1024), BF),...  122 us

profile of v4, /device:TPU:0, one launch (start us, length us, event | category | flops | bytes accessed | tf_op | source)
XLA Modules:
  0.0 125.1 jit_solution(4321676716449225091)
XLA Ops:
  1.3 122.2 %step.1 = (bf16[128,1024]{1,0:T(8,128)(2,1)}, f32[16,1024]{1,0:T(8,128)}) custom-call(bf16[2048,2048]{1,0:T(8,128)(2,1)} %bitcast.3, bf16[2048,1024]{1,0:T(8,128)(2,1)} %enc_h.1, bf16[1024,1024]{1,0:T(8,128)(2,1)} %self_h.1, bf16[1024,1024]{1,0:T(8,128)(2,1)} %neigh_h.1, bf16[1024,16,128]{2,1,0:T(8,128)(2,1)} %bitcast.4, bf16[128,1024]{1,0:T(8,128)(2,1)} %grad_h.1, ...), custom_call_target="tpu_custom_call" | custom-call | tf_op jit(solution)/shard_map/step/pallas_call | solution.py:607
  123.4 1.7 %hand_over.1 = (bf16[128,1024]{1,0:T(8,128)(2,1)}, f32[16,1024]{1,0:T(8,128)}) custom-call(bf16[128,1024]{1,0:T(8,128)(2,1)} %get-tuple-element.4.a, f32[16,1024]{1,0:T(8,128)} %get-tuple-element.5.b), custom_call_target="tpu_custom_call" | custom-call | tf_op jit(solution)/shard_map/hand_over/pallas_call | solution.py:621

commit v5 on v3

--- a/solution.py
+++ b/solution.py
@@ -536,7 +536,7 @@
         (pass_on, 1), (second_hop, 0), (first_hop, 2), (product, 3), (first_hop, 3),
         (second_hop, 1), (pass_on, 2), (raw, 0), (pass_on, 3), (second_hop, 2), (raw_z, 0),
         (raw, 1), (second_hop, 3), (raw_z, 1), (raw_x, 0), (raw, 2), (raw_z, 2), (raw_x, 1),
-        (raw_y, 0), (raw, 3), (raw_x, 2), (raw_y, 1), (raw_z, 3), (raw_y, 2), (raw_x, 3),
+        (raw_y, 0), (raw, 3), (raw_z, 3), (raw_x, 2), (raw_y, 1), (raw_y, 2), (raw_x, 3),
         (raw_y, 3),
     ):
         step(j)

time: 125 us -> 124 us (level)
  no operation moved by 1% of the time
where the time goes in v5:
time: 124 us
  Pallas kernels  123 us (99%)
  between operations  1.29 us (1%)
    pallas_call x1, Pallas kernels, local(): pl.pallas_call(kernel, out_shape=(jax.ShapeDtypeStruct((128, 1024), BF),...  121 us

profile of v5, /device:TPU:0, one launch (start us, length us, event | category | flops | bytes accessed | tf_op | source)
XLA Modules:
  0.0 123.8 jit_solution(4859201273567233356)
XLA Ops:
  1.3 120.8 %step.1 = (bf16[128,1024]{1,0:T(8,128)(2,1)}, f32[16,1024]{1,0:T(8,128)}) custom-call(bf16[2048,2048]{1,0:T(8,128)(2,1)} %bitcast.3, bf16[2048,1024]{1,0:T(8,128)(2,1)} %enc_h.1, bf16[1024,1024]{1,0:T(8,128)(2,1)} %self_h.1, bf16[1024,1024]{1,0:T(8,128)(2,1)} %neigh_h.1, bf16[1024,16,128]{2,1,0:T(8,128)(2,1)} %bitcast.4, bf16[128,1024]{1,0:T(8,128)(2,1)} %grad_h.1, ...), custom_call_target="tpu_custom_call" | custom-call | tf_op jit(solution)/shard_map/step/pallas_call | solution.py:607
  122.1 1.7 %hand_over.1 = (bf16[128,1024]{1,0:T(8,128)(2,1)}, f32[16,1024]{1,0:T(8,128)}) custom-call(bf16[128,1024]{1,0:T(8,128)(2,1)} %get-tuple-element.4.a, f32[16,1024]{1,0:T(8,128)} %get-tuple-element.5.b), custom_call_target="tpu_custom_call" | custom-call | tf_op jit(solution)/shard_map/hand_over/pallas_call | solution.py:621
